TPU v7x, 32 devices: a whole 2x2x4 slice. The times are simulated.
32 devices in a mesh: dom: 16 (over z, y, x), col: 2 (over core).
Axes of the slice: x: 2, y: 2, z: 4, core: 2. Of those that a mesh axis runs over, the one named last changes fastest.
Arguments:
- src_local: int32 [32768], P('dom'), may hold values from 0 to 4095
- dst_local: int32 [32768], P('dom'), may hold values from 0 to 4095
- edge_weight: float32 [32768], P('dom'), may hold values from 0.25 to 4
- send_counts: int32 [16, 16], P('dom'), may hold values from 1 to 128, as said below
- sketch: bfloat16 [128, 32768], P('col', 'dom'), may hold values from -6 to 6
Outputs:
- solution: float32 [128, 65536], P('col', 'dom')
- resistance: float32 [32768], P('dom')
Inputs may be any that keep to these rules, and one draw needn't show every extreme that they name: Each row of send_counts reaches 128 for some peer, and one peer receives 128 live slots from every partition.
All inputs are finite; a program needn't handle non-finite values.
Results may differ from a plain program's by a relative error of at most 0.0003.
Values sent between devices are 32-bit elements; how exact they have to be, the bound alone decides.
A program may use at most 64 MiB of HBM per device.

v0:
```python
import jax
import jax.numpy as jnp
from jax import lax
from jax.sharding import PartitionSpec as P

SKETCH = 128
VERT_DEV = 4096
SWEEPS = 3


ground_shift = 1.0
degree_boost = 0.25


def local(src_local, dst_local, edge_weight, send_counts, sketch):
    peers = lax.axis_size("dom")
    edges = src_local.shape[0]
    cap = edges // peers
    width = sketch.shape[0]
    live = (jnp.arange(cap)[None, :] < send_counts.reshape(peers, 1)).astype(jnp.float32)
    weight_live = edge_weight.reshape(peers, cap) * live
    flat_w = weight_live.reshape(-1)
    root = jnp.sqrt(flat_w)[None, :] * sketch.astype(jnp.float32)
    wanted = lax.all_to_all(
        dst_local.reshape(peers, cap), "dom", split_axis=0, concat_axis=0, tiled=True
    ).reshape(-1)
    arrived, arrived_w = (
        lax.all_to_all(
            root.reshape(width, peers, cap), "dom", split_axis=1, concat_axis=1, tiled=True
        ),
        lax.all_to_all(
            weight_live.reshape(1, peers, cap), "dom", split_axis=1, concat_axis=1, tiled=True
        ),
    )
    in_w = arrived_w.reshape(-1)
    zero_rows = jnp.zeros((width, VERT_DEV), jnp.float32)
    rhs = zero_rows.at[:, src_local].add(root).at[:, wanted].add(-arrived.reshape(width, -1))
    degree = jnp.zeros((VERT_DEV,), jnp.float32).at[src_local].add(flat_w).at[wanted].add(in_w)
    diag = (1.0 + degree_boost) * degree + ground_shift
    extra = degree_boost * degree + ground_shift

    def fetch(field):
        sent = field[:, wanted].reshape(width, peers, cap)
        return lax.all_to_all(sent, "dom", split_axis=1, concat_axis=1, tiled=True).reshape(
            width, -1
        )

    sigma = 1.25
    delta = 0.8
    coeff = 1.0 / sigma
    resid = rhs
    direction = resid / diag[None, :]
    solution = zero_rows
    for sweep in range(SWEEPS):
        solution = solution + direction
        if sweep < SWEEPS - 1:
            flow = flat_w[None, :] * (direction[:, src_local] - fetch(direction))
            back = lax.all_to_all(
                flow.reshape(width, peers, cap), "dom", split_axis=1, concat_axis=1, tiled=True
            ).reshape(width, -1)
            resid = resid - (
                zero_rows.at[:, src_local].add(flow).at[:, wanted].add(-back)
                + extra[None, :] * direction
            )
            newer = 1.0 / (2.0 * sigma - coeff)
            direction = newer * coeff * direction + 2.0 * newer / delta * resid / diag[None, :]
            coeff = newer
    diff = solution[:, src_local] - fetch(solution)
    partial_sum = jnp.sum(diff * diff, axis=0) * live.reshape(-1)
    resistance = lax.psum(partial_sum, "col") / SKETCH
    return (solution, resistance)


def solution(mesh):
    in_specs = (P("dom"), P("dom"), P("dom"), P("dom", None), P("col", "dom"))
    out_specs = (P("col", "dom"), P("dom"))
    return jax.shard_map(local, mesh=mesh, in_specs=in_specs, out_specs=out_specs, check_vma=False)
```

profile of v0, /device:TPU:0, one launch (start us, length us, event | category | flops | bytes accessed | tf_op | source)
XLA Modules:
  0.0 269.1 jit_solution(38351384684832800)
XLA Ops:
  2.0 8.3 %all-to-all-start.2 = ((f32[1,16,128]{2,0,1:T(1,128)}), f32[1,16,128]{2,0,1:T(1,128)S(1)}, u32[]{:S(2)}, u32[]{:S(2)}) async-start(f32[1,16,128]{2,0,1:T(1,128)} %compare_select_fusion.1), calls=%async_computation.2 | async-start | bytes 16384 | tf_op jit(solution)/shard_map/all_to_all | solution.py:31
  11.1 6.4 %all-to-all-done.2 = f32[1,16,128]{2,0,1:T(1,128)S(1)} async-done(((f32[1,16,128]{2,0,1:T(1,128)}), f32[1,16,128]{2,0,1:T(1,128)S(1)}, u32[]{:S(2)}, u32[]{:S(2)}) %all-to-all-start.2) | async-done | bytes 8224 | tf_op jit(solution)/shard_map/all_to_all | solution.py:31
  22.9 5.3 %all-to-all-done = s32[16,1,128]{2,1,0:T(1,128)S(1)} async-done(((s32[16,1,128]{2,1,0:T(1,128)}), s32[16,1,128]{2,1,0:T(1,128)S(1)}, u32[]{:S(2)}, u32[]{:S(2)}) %all-to-all-start) | async-done | bytes 8224 | tf_op jit(solution)/shard_map/all_to_all | solution.py:24
  33.1 11.2 %scatter_custom_fusion.2 = f32[4096]{0:T(1024)S(1)} fusion(s32[2048]{0:T(1024)S(1)} %get-tuple-element.20, f32[2048]{0:T(1024)S(1)} %get-tuple-element.14, f32[]{:T(128)} %constant.11.clone.1), kind=kCustom, calls=%fused_computation.48 | custom fusion | flops 2048 | bytes 16388 | tf_op jit(solution)/shard_map/scatter-add | solution.py:38
  44.4 12.3 %scatter_custom_fusion = f32[64,4096]{0,1:T(8,128)S(1)} fusion(s32[2048]{0:T(1024)S(1)} %get-tuple-element.20, f32[2048,64]{1,0:T(8,128)} %copy.20, f32[]{:T(128)} %constant.11.clone.1), kind=kCustom, calls=%fused_computation.27 | custom fusion | flops 131072 | bytes 1049088 | tf_op jit(solution)/shard_map/scatter-add | solution.py:37
  56.7 11.5 %scatter_fusion.1 = f32[4096]{0:T(1024)S(1)} fusion(f32[4096]{0:T(1024)S(1)} %scatter_custom_fusion.2, s32[2048]{0:T(1024)S(1)} %bitcast.85, f32[2048]{0:T(1024)S(1)} %bitcast.92), kind=kCustom, calls=%fused_computation.9 | custom fusion | flops 2048 | bytes 32768 | tf_op jit(solution)/shard_map/scatter-add | solution.py:38
  70.5 12.2 %scatter_fusion = f32[64,4096]{0,1:T(8,128)S(1)} fusion(f32[64,4096]{0,1:T(8,128)S(1)} %scatter_custom_fusion, s32[2048]{0:T(1024)S(1)} %bitcast.87, f32[2048,64]{1,0:T(8,128)S(1)} %copy.23), kind=kCustom, calls=%fused_computation.7 | custom fusion | flops 131072 | bytes 1581056 | tf_op jit(solution)/shard_map/scatter-add | solution.py:37
  84.1 4.9 %broadcast_multiply_fusion.1 = (f32[64,4096]{0,1:T(8,128)}, f32[64,4096]{0,1:T(8,128)S(1)}) fusion(f32[4096]{0:T(1024)S(1)} %get-tuple-element.18, f32[64,4096]{0,1:T(8,128)} %copy-done.1, f32[4096]{0:T(1024)S(1)} %get-tuple-element.17), kind=kLoop, calls=%fused_computation.25 | loop fusion | flops 524288 | bytes 3178496 | tf_op jit(solution)/shard_map/mul | solution.py:63
  89.0 5.5 %gather_fusion.1 = f32[2048,64]{1,0:T(8,128)S(1)} fusion(f32[64,4096]{0,1:T(8,128)S(1)} %get-tuple-element.12, s32[2048]{0:T(1024)S(1)} %broadcast_clamp_fusion), kind=kCustom, calls=%fused_computation.1 | custom fusion | bytes 1056768 | tf_op jit(solution)/shard_map/gather | solution.py:43
  95.6 6.9 %all-to-all-start.3 = ((f32[64,16,128]{2,0,1:T(8,128)}), f32[64,16,128]{2,0,1:T(8,128)}, u32[]{:S(2)}, u32[]{:S(2)}) async-start(f32[64,16,128]{2,0,1:T(8,128)} %copy.24), calls=%async_computation.3 | async-start | bytes 1048576 | tf_op jit(solution)/shard_map/all_to_all | solution.py:44
  102.5 5.5 %gather_fusion = f32[2048,64]{1,0:T(8,128)S(1)} fusion(f32[64,4096]{0,1:T(8,128)S(1)} %get-tuple-element.12, s32[2048]{0:T(1024)S(1)} %get-tuple-element.19), kind=kCustom, calls=%fused_computation | custom fusion | bytes 1056768 | tf_op jit(solution)/shard_map/gather | solution.py:57
  109.1 5.7 %all-to-all-done.3 = f32[64,16,128]{2,0,1:T(8,128)} async-done(((f32[64,16,128]{2,0,1:T(8,128)}), f32[64,16,128]{2,0,1:T(8,128)}, u32[]{:S(2)}, u32[]{:S(2)}) %all-to-all-start.3) | async-done | bytes 524320 | tf_op jit(solution)/shard_map/all_to_all | solution.py:44
  126.3 14.8 %scatter_custom_fusion.4 = f32[64,4096]{0,1:T(8,128)} fusion(f32[64,4096]{0,1:T(8,128)} %get-tuple-element.11, s32[2048]{0:T(1024)S(1)} %get-tuple-element.20, f32[64,2048]{0,1:T(8,128)} %fusion.5), kind=kCustom, calls=%fused_computation.20 | custom fusion | flops 131072 | bytes 2097152 | tf_op jit(solution)/shard_map/scatter-add | solution.py:62
  144.4 13.3 %scatter_fusion.2 = f32[64,4096]{0,1:T(8,128)} fusion(f32[64,4096]{0,1:T(8,128)} %scatter_custom_fusion.4, s32[2048]{0:T(1024)S(1)} %bitcast.88, f32[2048,64]{1,0:T(8,128)S(1)} %copy.28), kind=kCustom, calls=%fused_computation.11 | custom fusion | flops 131072 | bytes 1581056 | tf_op jit(solution)/shard_map/scatter-add | solution.py:62
  162.3 7.0 %gather_fusion.3 = f32[2048,64]{1,0:T(8,128)S(1)} fusion(f32[64,4096]{0,1:T(8,128)} %get-tuple-element.9, s32[2048]{0:T(1024)S(1)} %broadcast_clamp_fusion), kind=kCustom, calls=%fused_computation.3 | custom fusion | bytes 1056768 | tf_op jit(solution)/shard_map/gather | solution.py:43
  170.4 6.7 %all-to-all-start.5 = ((f32[64,16,128]{2,0,1:T(8,128)}), f32[64,16,128]{2,0,1:T(8,128)}, u32[]{:S(2)}, u32[]{:S(2)}) async-start(f32[64,16,128]{2,0,1:T(8,128)} %copy.29), calls=%async_computation.5 | async-start | bytes 1048576 | tf_op jit(solution)/shard_map/all_to_all | solution.py:44
  177.1 7.1 %gather_fusion.2 = f32[2048,64]{1,0:T(8,128)S(1)} fusion(f32[64,4096]{0,1:T(8,128)} %get-tuple-element.9, s32[2048]{0:T(1024)S(1)} %get-tuple-element.19), kind=kCustom, calls=%fused_computation.2 | custom fusion | bytes 1056768 | tf_op jit(solution)/shard_map/gather | solution.py:57
  185.4 4.6 %all-to-all-done.5 = f32[64,16,128]{2,0,1:T(8,128)} async-done(((f32[64,16,128]{2,0,1:T(8,128)}), f32[64,16,128]{2,0,1:T(8,128)}, u32[]{:S(2)}, u32[]{:S(2)}) %all-to-all-start.5) | async-done | bytes 524320 | tf_op jit(solution)/shard_map/all_to_all | solution.py:44
  201.3 14.8 %scatter_custom_fusion.6 = f32[64,4096]{0,1:T(8,128)} fusion(f32[64,4096]{0,1:T(8,128)} %get-tuple-element.8, s32[2048]{0:T(1024)S(1)} %get-tuple-element.20, f32[64,2048]{0,1:T(8,128)} %fusion.2), kind=kCustom, calls=%fused_computation.16 | custom fusion | flops 131072 | bytes 2097152 | tf_op jit(solution)/shard_map/scatter-add | solution.py:62
  219.3 13.2 %scatter_fusion.3 = f32[64,4096]{0,1:T(8,128)} fusion(f32[64,4096]{0,1:T(8,128)} %scatter_custom_fusion.6, s32[2048]{0:T(1024)S(1)} %bitcast.89, f32[2048,64]{1,0:T(8,128)S(1)} %copy.33), kind=kCustom, calls=%fused_computation.13 | custom fusion | flops 131072 | bytes 1581056 | tf_op jit(solution)/shard_map/scatter-add | solution.py:62
  236.7 7.0 %gather_fusion.5 = f32[2048,64]{1,0:T(8,128)S(1)} fusion(f32[64,4096]{0,1:T(8,128)} %add_add_fusion, s32[2048]{0:T(1024)S(1)} %broadcast_clamp_fusion), kind=kCustom, calls=%fused_computation.5 | custom fusion | bytes 1056768 | tf_op jit(solution)/shard_map/gather | solution.py:43
  244.9 6.9 %all-to-all-start.7 = ((f32[64,16,128]{2,0,1:T(8,128)}), f32[64,16,128]{2,0,1:T(8,128)}, u32[]{:S(2)}, u32[]{:S(2)}) async-start(f32[64,16,128]{2,0,1:T(8,128)} %copy.34), calls=%async_computation.7 | async-start | bytes 1048576 | tf_op jit(solution)/shard_map/all_to_all | solution.py:44
  251.8 5.5 %gather_fusion.4 = f32[2048,64]{1,0:T(8,128)S(1)} fusion(f32[64,4096]{0,1:T(8,128)S(1)} %copy-done, s32[2048]{0:T(1024)S(1)} %get-tuple-element.19), kind=kCustom, calls=%fused_computation.4 | custom fusion | bytes 1056768 | tf_op jit(solution)/shard_map/gather | solution.py:68
  259.2 5.6 %all-to-all-done.7 = f32[64,16,128]{2,0,1:T(8,128)} async-done(((f32[64,16,128]{2,0,1:T(8,128)}), f32[64,16,128]{2,0,1:T(8,128)}, u32[]{:S(2)}, u32[]{:S(2)}) %all-to-all-start.7) | async-done | bytes 524320 | tf_op jit(solution)/shard_map/all_to_all | solution.py:44
  (49 shorter events, 65.7 us)
Async XLA Ops:
  0.6 31.1 %copy-start.2 = (s32[2048]{0:T(1024)S(1)}, s32[2048]{0:T(1024)}, u32[]{:S(2)}) copy-start(s32[2048]{0:T(1024)} %param.5) | copy-start | bytes 24580
  2.0 15.5 %all-to-all-start.2 = ((f32[1,16,128]{2,0,1:T(1,128)}), f32[1,16,128]{2,0,1:T(1,128)S(1)}, u32[]{:S(2)}, u32[]{:S(2)}) async-start(f32[1,16,128]{2,0,1:T(1,128)} %compare_select_fusion.1), calls=%async_computation.2 | async-start | bytes 16384 | tf_op jit(solution)/shard_map/all_to_all | solution.py:31
  17.5 10.6 %all-to-all-start = ((s32[16,1,128]{2,1,0:T(1,128)}), s32[16,1,128]{2,1,0:T(1,128)S(1)}, u32[]{:S(2)}, u32[]{:S(2)}) async-start(s32[16,1,128]{2,1,0:T(1,128)} %bitcast.94), calls=%async_computation | async-start | bytes 16384 | tf_op jit(solution)/shard_map/all_to_all | solution.py:24
  28.2 40.1 %all-to-all-start.1 = ((f32[64,16,128]{2,0,1:T(8,128)}), f32[64,16,128]{2,0,1:T(8,128)S(1)}, u32[]{:S(2)}, u32[]{:S(2)}) async-start(f32[64,16,128]{2,0,1:T(8,128)} %bitcast.78), calls=%async_computation.1 | async-start | bytes 1048576 | tf_op jit(solution)/shard_map/all_to_all | solution.py:28
  82.7 1.4 copy-start.1
  95.6 19.3 %all-to-all-start.3 = ((f32[64,16,128]{2,0,1:T(8,128)}), f32[64,16,128]{2,0,1:T(8,128)}, u32[]{:S(2)}, u32[]{:S(2)}) async-start(f32[64,16,128]{2,0,1:T(8,128)} %copy.24), calls=%async_computation.3 | async-start | bytes 1048576 | tf_op jit(solution)/shard_map/all_to_all | solution.py:44
  117.0 24.2 %all-to-all-start.4 = ((f32[64,16,128]{2,0,1:T(8,128)}), f32[64,16,128]{2,0,1:T(8,128)}, u32[]{:S(2)}, u32[]{:S(2)}) async-start(f32[64,16,128]{2,0,1:T(8,128)} %subtract_multiply_fusion.1), calls=%async_computation.4 | async-start | bytes 1048576 | tf_op jit(solution)/shard_map/all_to_all | solution.py:58
  170.4 19.6 %all-to-all-start.5 = ((f32[64,16,128]{2,0,1:T(8,128)}), f32[64,16,128]{2,0,1:T(8,128)}, u32[]{:S(2)}, u32[]{:S(2)}) async-start(f32[64,16,128]{2,0,1:T(8,128)} %copy.29), calls=%async_computation.5 | async-start | bytes 1048576 | tf_op jit(solution)/shard_map/all_to_all | solution.py:44
  192.1 23.9 %all-to-all-start.6 = ((f32[64,16,128]{2,0,1:T(8,128)}), f32[64,16,128]{2,0,1:T(8,128)}, u32[]{:S(2)}, u32[]{:S(2)}) async-start(f32[64,16,128]{2,0,1:T(8,128)} %subtract_multiply_fusion), calls=%async_computation.6 | async-start | bytes 1048576 | tf_op jit(solution)/shard_map/all_to_all | solution.py:58
  243.8 8.0 %copy-start = (f32[64,4096]{0,1:T(8,128)S(1)}, f32[64,4096]{0,1:T(8,128)}, u32[]{:S(2)}) copy-start(f32[64,4096]{0,1:T(8,128)} %add_add_fusion) | copy-start | bytes 3145732
  244.9 19.9 %all-to-all-start.7 = ((f32[64,16,128]{2,0,1:T(8,128)}), f32[64,16,128]{2,0,1:T(8,128)}, u32[]{:S(2)}, u32[]{:S(2)}) async-start(f32[64,16,128]{2,0,1:T(8,128)} %copy.34), calls=%async_computation.7 | async-start | bytes 1048576 | tf_op jit(solution)/shard_map/all_to_all | solution.py:44
  258.9 7.1 %copy-start.3 = (s32[1,16]{1,0:T(1,128)S(1)}, s32[1,16]{1,0:T(1,128)}, u32[]{:S(2)}) copy-start(s32[1,16]{1,0:T(1,128)} %param.8) | copy-start | bytes 196
where the time goes:
time: 271 us; the launch traced here: 269 us
  other arithmetic  136 us (50%)
  local copies, waits for them, and re-layouts  57.4 us (21%)
  starting transfers between devices  44.5 us (16%)
  waiting for transfers between devices  27.7 us (10%)
    scatter-add x4, other arithmetic, local(): zero_rows.at[:, src_local].add(flow).at[:, wanted].add(-back)  56.1 us
    scatter-add x2, other arithmetic, local(): zero_rows.at[:, src_local].add(root).at[:, wanted]  24.6 us
    scatter-add x2, other arithmetic, local(): jnp.zeros((VERT_DEV,), jnp.float32).at[src_local].add(flat_w).at[wanted]  22.8 us
    all_to_all x3, starting transfers between devices, fetch(): lax.all_to_all(sent, 'dom', split_axis=1, concat_axis=1, tiled=True)  20.5 us
    gather x3, local copies, waits for them, and re-layouts, fetch(): sent = field[:, wanted].reshape(width, peers, cap)  19.6 us
    all_to_all x3, waiting for transfers between devices, fetch(): lax.all_to_all(sent, 'dom', split_axis=1, concat_axis=1, tiled=True)  16 us
    gather x4, local copies, waits for them, and re-layouts, local(): flow = flat_w[None, :] * (direction[:, src_local] - fetch(direction))  14.8 us
    mul x2, other arithmetic, local(): extra[None, :] * direction  9.55 us
  transfers between devices with their start and end apart: 8, of which 5 were waited for; matrix products, arithmetic and copies ran while one was open for 37% of the time, Pallas kernels for 0%

commit v1 on v0

v1 whole, which is shorter than its diff:
```python
import functools

import jax
import jax.numpy as jnp
from jax import lax
from jax.experimental import pallas as pl
from jax.experimental.pallas import tpu as pltpu
from jax.sharding import PartitionSpec as P

MESH = pl.DeviceIdType.MESH
F32 = jnp.float32
BF16 = jnp.bfloat16
VERT_DEV = 4096
SKETCH = 128
SWEEPS = 3
LANES = 128
HALF = 64
ground_shift = 1.0
degree_boost = 0.25


def either(a, b, n):
    total, bit = 0, 1
    while bit < n:
        total = total + bit * lax.rem(lax.div(a, bit) + lax.div(b, bit), 2)
        bit *= 2
    return total


def kernel(
    peers, cap, meta_ref, root_ref, src_ref, weight_ref, live_ref, sol_ref, res_ref,
    same, ids, rows, acc, field, resid, total, inv, keep, wide, ends, part, part_in,
    meta_in, root_in, one_in, two_in, last_out, last_in,
    meta_s, meta_r, even_s, even_r, odd_s, odd_r, part_s, part_r,
):
    me = lax.axis_index("dom")
    other = 1 - lax.axis_index("col")
    group = LANES // cap
    count = peers // group
    own_group = lax.div(me, group)

    barrier = pltpu.get_barrier_semaphore()

    def greet(i, _):
        pl.semaphore_signal(barrier, inc=1, device_id={"dom": either(me, i, peers)}, device_id_type=MESH)
        return 0

    lax.fori_loop(1, peers, greet, 0)
    pl.semaphore_signal(barrier, inc=1, device_id={"col": other}, device_id_type=MESH)
    pl.semaphore_wait(barrier, peers)

    def copy(p, source, target, s, r):
        return pltpu.make_async_remote_copy(
            src_ref=source.at[p], dst_ref=target.at[me], send_sem=s.at[p], recv_sem=r.at[me],
            device_id={"dom": p}, device_id_type=MESH,
        )

    def arrival(p, source, target, s, r):
        return pltpu.make_async_remote_copy(
            src_ref=source.at[p], dst_ref=target.at[p], send_sem=s.at[p], recv_sem=r.at[p],
            device_id={"dom": p}, device_id_type=MESH,
        )

    def send_group(far, source, target, s, r):
        for j in range(group):
            i = far * group + j
            p = either(me, i, peers)

            @pl.when(i != 0)
            def _():
                copy(p, source, target, s, r).start()

            @pl.when(i == 0)
            def _():
                target[me] = source[me]

    def wait_group(far, source, target, s, r):
        for j in range(group):
            i = far * group + j
            p = either(me, i, peers)

            @pl.when(i != 0)
            def _():
                arrival(p, source, target, s, r).wait_recv()

    def wait_sent(source, target, s, r):
        def step(i, _):
            copy(either(me, i, peers), source, target, s, r).wait_send()
            return 0

        lax.fori_loop(1, peers, step, 0)

    low = lax.broadcasted_iota(jnp.int32, (LANES, LANES), 1) < HALF

    def mask(a):
        return low[: a.shape[0]]

    def turned(a):
        return pltpu.roll(a, HALF, axis=1)

    def doubled(a):
        b = turned(a)
        return jnp.where(mask(a), a, b), jnp.where(mask(a), b, a)

    def split(a):
        high = a.astype(BF16).astype(F32)
        return jnp.where(low, high, a - high).astype(BF16)

    def column(row):
        return jnp.broadcast_to(row, (LANES, LANES)).T

    def unfold(ref, g):
        pieces = []
        for j in range(group):
            pieces.extend(doubled(ref[g * group + j]))
        return jnp.concatenate(pieces, axis=0)

    def block(ref, g):
        return ref[pl.ds(g * group, group)].reshape(LANES, LANES)

    def near_first(t):
        return either(own_group, lax.rem(count - t, count), count), lax.rem(count - t, count)

    def send_meta(t, _):
        send_group(count - 1 - t, meta_ref, meta_in, meta_s, meta_r)
        return 0

    lax.fori_loop(0, count, send_meta, 0)

    def send_root(t, _):
        send_group(count - 1 - t, root_ref, root_in, even_s, even_r)
        return 0

    lax.fori_loop(0, count, send_root, 0)

    def first_ends(g, _):
        row = src_ref[pl.ds(g, 1), :]
        rows[g, 0:1] = row
        ids[g] = column(row)
        wide[g] = column(weight_ref[pl.ds(g, 1), :])
        return 0

    lax.fori_loop(0, count, first_ends, 0)

    def second_ends(t, _):
        g, far = near_first(t)
        wait_group(far, meta_ref, meta_in, meta_s, meta_r)
        named = [column(meta_in[g * group + j][0:1])[:cap] for j in range(group)]
        named = jnp.concatenate(named, axis=0)
        heavy = [column(meta_in[g * group + j][1:2])[:cap] for j in range(group)]
        heavy = jnp.concatenate(heavy, axis=0)
        ids[count + g] = named
        rows[g, 1:2] = named.T[0:1]
        wide[count + g] = heavy
        return 0

    lax.fori_loop(0, count, second_ends, 0)

    tile = 512
    blocks = tile // LANES
    tiles = 2 * count // blocks

    acc[...] = jnp.zeros_like(acc)

    def first_product(t, _):
        g, far = near_first(t)
        wait_group(far, root_ref, root_in, even_s, even_r)
        value = jnp.concatenate([split(unfold(root_ref, g)), split(-unfold(root_in, g))], axis=0)
        load = jnp.concatenate([split(wide[g]), split(wide[count + g])], axis=0)
        x = jnp.concatenate([value, load], axis=1)
        row_u, row_v = rows[g, 0:1], rows[g, 1:2]

        def step(k, _):
            at = pl.ds(pl.multiple_of(k * tile, tile), tile)
            name = ids[pl.ds(k * blocks, blocks)].reshape(tile, LANES)
            e = jnp.concatenate(
                [jnp.where(name == row_u, 1.0, 0.0), jnp.where(name == row_v, 1.0, 0.0)], axis=1
            ).astype(BF16)
            same[g, at, :] = e
            acc[at, :] += jnp.dot(e, x, preferred_element_type=F32)
            return 0

        lax.fori_loop(0, tiles, step, 0)
        return 0

    lax.fori_loop(0, count, first_product, 0)
    wait_sent(meta_ref, meta_in, meta_s, meta_r)
    wait_sent(root_ref, root_in, even_s, even_r)

    def at_ends(g, lane):
        a = acc[pl.ds(pl.multiple_of(g * LANES, LANES), LANES), lane : lane + LANES]
        b = acc[pl.ds(pl.multiple_of((count + g) * LANES, LANES), LANES), lane : lane + LANES]
        return jnp.where(low, a + turned(a), b + turned(b))

    def put(ref, g, value):
        ref[pl.ds(g * group, group)] = value.reshape(group, cap, LANES)

    def start_field(t, _):
        far = count - 1 - t
        g = either(own_group, far, count)
        degree = at_ends(g, LANES)
        one_over = 1.0 / ((1.0 + degree_boost) * degree + ground_shift)
        inv[g] = one_over
        keep[g] = (degree_boost * degree + ground_shift) * one_over
        d = at_ends(g, 0) * one_over
        put(field, g, d)
        send_group(far, field, one_in, odd_s, odd_r)
        resid[g] = d
        total[g] = d
        wide[g] = jnp.where(low, wide[g], wide[count + g])
        return 0

    lax.fori_loop(0, count, start_field, 0)

    def multiply(came, s, r):
        acc[:, 0:LANES] = jnp.zeros((2 * count * LANES, LANES), F32)

        def product(t, _):
            g, far = near_first(t)
            wait_group(far, field, came, s, r)
            flow = wide[g] * (block(field, g) - turned(block(came, g)))
            flow_u, flow_v = doubled(flow)
            x = jnp.concatenate([split(flow_u), split(flow_v)], axis=0)

            def step(k, _):
                at = pl.ds(pl.multiple_of(k * tile, tile), tile)
                acc[at, 0:LANES] += jnp.dot(same[g, at, :], x, preferred_element_type=F32)
                return 0

            lax.fori_loop(0, tiles, step, 0)
            return 0

        lax.fori_loop(0, count, product, 0)
        wait_sent(field, came, s, r)

    sigma, delta = 1.25, 0.8
    coeff = 1.0 / sigma
    newer = 1.0 / (2.0 * sigma - coeff)
    pairs = ((newer * coeff, 2.0 * newer / delta),)
    coeff = newer
    newer = 1.0 / (2.0 * sigma - coeff)
    pairs += ((newer * coeff, 2.0 * newer / delta),)

    multiply(one_in, odd_s, odd_r)

    def second_field(t, _):
        far = count - 1 - t
        g = either(own_group, far, count)
        d = block(field, g)
        r = resid[g] - (at_ends(g, 0) * inv[g] + keep[g] * d)
        d = pairs[0][0] * d + pairs[0][1] * r
        put(field, g, d)
        send_group(far, field, two_in, even_s, even_r)
        resid[g] = r
        total[g] = total[g] + d
        return 0

    lax.fori_loop(0, count, second_field, 0)
    multiply(two_in, even_s, even_r)

    def third_field(t, _):
        far = count - 1 - t
        g = either(own_group, far, count)
        d = block(field, g)
        r = resid[g] - (at_ends(g, 0) * inv[g] + keep[g] * d)
        d = pairs[1][0] * d + pairs[1][1] * r
        whole = total[g] + d
        total[g] = whole
        for j in range(group):
            a = whole[j * cap : j * cap + cap // 2]
            b = whole[j * cap + cap // 2 : (j + 1) * cap]
            last_out[g * group + j] = jnp.where(mask(a), turned(a), b)
        send_group(far, last_out, last_in, odd_s, odd_r)
        whole_u, whole_v = doubled(whole)
        ones = jnp.ones((LANES, LANES), BF16)
        ends[g, 0:LANES, :] = jnp.concatenate([split(whole_u), ones], axis=1)
        ends[g, LANES:, :] = jnp.concatenate([split(whole_v), ones], axis=1)
        return 0

    lax.fori_loop(0, count, third_field, 0)

    strip = 256

    def vertices(k, _):
        first = k * strip
        name = (lax.broadcasted_iota(jnp.int32, (strip, LANES), 0) + first).astype(F32)
        out = jnp.zeros((strip, 2 * LANES), F32)
        for g in range(count):
            e = jnp.concatenate(
                [jnp.where(name == rows[g, 0:1], 1.0, 0.0), jnp.where(name == rows[g, 1:2], 1.0, 0.0)], axis=1
            ).astype(BF16)
            out = out + jnp.dot(e, ends[g], preferred_element_type=F32)
        value = out[:, 0:LANES]
        value = (value + turned(value)) / jnp.maximum(out[:, LANES:], 1.0)
        sol_ref[:, pl.ds(pl.multiple_of(first, strip), strip)] = value.T[0:HALF]
        return 0

    lax.fori_loop(0, VERT_DEV // strip, vertices, 0)

    def differences(t, _):
        g, far = near_first(t)
        wait_group(far, last_out, last_in, odd_s, odd_r)
        diff = jnp.where(low, total[g] - unfold(last_in, g), 0.0)
        part[pl.ds(g, 1), :] = jnp.sum((diff * diff).T, axis=0, keepdims=True)
        return 0

    lax.fori_loop(0, count, differences, 0)
    wait_sent(last_out, last_in, odd_s, odd_r)

    swap = pltpu.make_async_remote_copy(
        src_ref=part, dst_ref=part_in, send_sem=part_s, recv_sem=part_r,
        device_id={"col": other}, device_id_type=MESH,
    )
    swap.start()
    swap.wait()
    res_ref[...] = (part[...] + part_in[...]) / SKETCH * live_ref[...]


def local(src_local, dst_local, edge_weight, send_counts, sketch):
    peers = lax.axis_size("dom")
    edges = src_local.shape[0]
    cap = edges // peers
    width = sketch.shape[0]
    count = edges // LANES
    live = (jnp.arange(cap)[None, :] < send_counts.reshape(peers, 1)).astype(F32)
    weight = edge_weight.reshape(peers, cap) * live
    root = (jnp.sqrt(weight).reshape(1, edges) * sketch.astype(F32)).reshape(width, peers, 2, cap // 2)
    root = root.transpose(1, 3, 2, 0).reshape(peers, cap // 2, LANES)
    meta = jnp.stack([dst_local.reshape(peers, cap).astype(F32), weight], axis=1)
    meta = jnp.pad(meta, ((0, 0), (0, 6), (0, LANES - cap)))
    vmem = functools.partial(pl.BlockSpec, memory_space=pltpu.VMEM)
    dma = pltpu.SemaphoreType.DMA
    wide = pltpu.VMEM((count, LANES, LANES), F32)
    whole = pltpu.VMEM((peers, cap, LANES), F32)
    half = pltpu.VMEM((peers, cap // 2, LANES), F32)
    solution, resistance = pl.pallas_call(
        functools.partial(kernel, peers, cap),
        out_shape=(jax.ShapeDtypeStruct((width, VERT_DEV), F32), jax.ShapeDtypeStruct((count, LANES), F32)),
        in_specs=[vmem()] * 5,
        out_specs=(vmem(), vmem()),
        scratch_shapes=[
            pltpu.VMEM((count, 2 * edges, 2 * LANES), BF16),
            pltpu.VMEM((2 * count, LANES, LANES), F32),
            pltpu.VMEM((count, 8, LANES), F32),
            pltpu.VMEM((2 * edges, 2 * LANES), F32),
            whole, wide, wide, wide, wide,
            pltpu.VMEM((2 * count, LANES, LANES), F32),
            pltpu.VMEM((count, 2 * LANES, 2 * LANES), BF16),
            pltpu.VMEM((count, LANES), F32),
            pltpu.VMEM((count, LANES), F32),
            pltpu.VMEM((peers, 8, LANES), F32),
            half, whole, whole, half, half,
            dma((peers,)), dma((peers,)), dma((peers,)), dma((peers,)), dma((peers,)), dma((peers,)),
            dma, dma,
        ],
        compiler_params=pltpu.CompilerParams(
            collective_id=0, has_side_effects=True, vmem_limit_bytes=60 * 1024 * 1024
        ),
    )(meta, root, src_local.astype(F32).reshape(count, LANES), weight.reshape(count, LANES), live.reshape(count, LANES))
    return solution, resistance.reshape(edges)


def solution(mesh):
    in_specs = (P("dom"), P("dom"), P("dom"), P("dom", None), P("col", "dom"))
    out_specs = (P("col", "dom"), P("dom"))
    return jax.shard_map(local, mesh=mesh, in_specs=in_specs, out_specs=out_specs, check_vma=False)
```

time: 271 us -> 173 us (0.64)
  Pallas kernels: 0 us -> 159 us
  other arithmetic: 136 us -> 4.42 us
  local copies, waits for them, and re-layouts: 57.4 us -> 7.92 us
  starting transfers between devices: 44.5 us -> 0 us
  waiting for transfers between devices: 27.7 us -> 0 us
    pallas_call x0 -> x1, Pallas kernels: none -> 159 us  [local(): pl.pallas_call(functools.partial(kernel, peers, cap), out_shape=(jax.Shap...]
    scatter-add x8 -> x0, other arithmetic: 103 us -> none  [the longest x4 56.1 us: local(): zero_rows.at[:, src_local].add(flow).at[:, wanted].add(-back)]
    all_to_all x8 -> x0, starting transfers between devices: 44.5 us -> none  [the longest x3 20.5 us: fetch(): lax.all_to_all(sent, 'dom', split_axis=1, concat_axis=1, tiled=True)]
    gather x9 -> x0, local copies, waits for them, and re-layouts: 40.1 us -> none  [the longest x3 19.6 us: fetch(): sent = field[:, wanted].reshape(width, peers, cap)]
    all_to_all x8 -> x0, waiting for transfers between devices: 27.7 us -> none  [the longest x3 16 us: fetch(): lax.all_to_all(sent, 'dom', split_axis=1, concat_axis=1, tiled=True)]
    mul x8 -> x3, other arithmetic: 20.3 us -> 1.74 us  [the longest x1 0.99 us: local(): jnp.sqrt(weight).reshape(1, edges) * sketch.astype(F32)]
    all_to_all x2 -> x0, local copies, waits for them, and re-layouts: 4.71 us -> none  [fetch(): lax.all_to_all(sent, 'dom', split_axis=1, concat_axis=1, tiled=True)]
    neg x3 -> x0, other arithmetic: 4.59 us -> none  [the longest x2 3.76 us: local(): -back]
  transfers between devices with their start and end apart: 8 -> 0, of which waited for: 5 -> 0; matrix products, arithmetic and copies ran while one was open for 37% -> 0% of each run, Pallas kernels for 0% -> 0%
where the time goes in v1:
time: 173 us; the launch traced here: 172 us
  Pallas kernels  159 us (92%)
  local copies, waits for them, and re-layouts  7.92 us (5%)
  other arithmetic  4.42 us (3%)
    pallas_call x1, Pallas kernels, local(): pl.pallas_call(functools.partial(kernel, peers, cap), out_shape=(jax.Shap...  159 us
    unnamed x12, local copies, waits for them, and re-layouts  4.17 us

profile of v1, /device:TPU:0, one launch (start us, length us, event | category | flops | bytes accessed | tf_op | source)
XLA Modules:
  0.0 172.4 jit_solution(10633777505248960829)
XLA Ops:
  0.6 0.0 copy-start.1
  0.6 0.6 copy-done.1
  1.3 0.8 select_sqrt_fusion
  2.1 1.0 convert_multiply_fusion
  3.1 0.8 reshape.98
  3.8 1.6 copy.7
  5.4 0.0 copy-start
  5.4 1.4 reshape.99.root_ref
  6.8 0.0 copy-done
  6.8 0.0 copy-start.2
  6.8 0.1 compare_select_fusion
  6.9 0.6 copy-done.2
  7.5 0.6 select_maximum_fusion.meta_ref
  8.2 0.7 bitcast_select_fusion.weight_ref
  8.8 0.0 copy-start.3
  8.8 0.7 fusion.live_ref
  9.5 0.0 copy-done.3
  9.5 0.6 convert_bitcast_fusion.src_ref
  10.1 159.4 %shard_map.68 = (f32[64,4096]{1,0:T(8,128)}, f32[16,128]{1,0:T(8,128)}) custom-call(f32[16,8,128]{2,1,0:T(8,128)} %select_maximum_fusion.meta_ref, f32[16,64,128]{2,1,0:T(8,128)} %reshape.99.root_ref, f32[16,128]{1,0:T(8,128)} %convert_bitcast_fusion.src_ref, f32[16,128]{1,0:T(8,128)} %bitcast_select_fusion.weight_ref, f32[16,128]{1,0:T(8,128)} %fusion.live_ref), custom_call_target="tpu_custom_call" | custom-call | tf_op jit(solution)/shard_map/pallas_call | solution.py:336
  169.5 0.0 copy-start.4
  169.5 2.3 %copy.10 = f32[64,4096]{1,0:T(8,128)} copy(f32[64,4096]{1,0:T(8,128)} %get-tuple-element.8) | data formatting | bytes 2097152
  171.8 0.0 copy-done.4
  171.8 0.6 copy.11
  (1 shorter events, 0.0 us)
Async XLA Ops:
  0.6 0.7 copy-start.1
  5.4 1.4 copy-start
  6.8 0.7 copy-start.2
  8.8 0.7 copy-start.3
  169.5 2.3 %copy-start.4 = (f32[16,128]{1,0:T(8,128)S(1)}, f32[16,128]{1,0:T(8,128)}, u32[]{:S(2)}) copy-start(f32[16,128]{1,0:T(8,128)} %get-tuple-element.5) | copy-start | bytes 24580

commit v2 on v1

--- a/solution.py
+++ b/solution.py
@@ -28,9 +28,9 @@
 
 
 def kernel(
-    peers, cap, meta_ref, root_ref, src_ref, weight_ref, live_ref, sol_ref, res_ref,
+    peers, cap, counts_ref, src_ref, dst_ref, flat_ref, weight_ref, sketch_ref, sol_ref, res_ref,
     same, ids, rows, acc, field, resid, total, inv, keep, wide, ends, part, part_in,
-    meta_in, root_in, one_in, two_in, last_out, last_in,
+    live_ref, meta_ref, root_ref, meta_in, root_in, one_in, two_in, last_out, last_in,
     meta_s, meta_r, even_s, even_r, odd_s, odd_r, part_s, part_r,
 ):
     me = lax.axis_index("dom")
@@ -47,7 +47,6 @@
 
     lax.fori_loop(1, peers, greet, 0)
     pl.semaphore_signal(barrier, inc=1, device_id={"col": other}, device_id_type=MESH)
-    pl.semaphore_wait(barrier, peers)
 
     def copy(p, source, target, s, r):
         return pltpu.make_async_remote_copy(
@@ -121,6 +120,18 @@
     def near_first(t):
         return either(own_group, lax.rem(count - t, count), count), lax.rem(count - t, count)
 
+    spot = lax.broadcasted_iota(jnp.int32, (1, LANES), 1)
+
+    def message(p, _):
+        alive = jnp.where(spot[:, :cap] < counts_ref[0, p], 1.0, 0.0)
+        meta_ref[p, 0:1, 0:cap] = dst_ref[pl.ds(p, 1), :].astype(F32)
+        meta_ref[p, 1:2, 0:cap] = flat_ref[pl.ds(p, 1), :] * alive
+        return 0
+
+    meta_ref[...] = jnp.zeros_like(meta_ref)
+    lax.fori_loop(0, peers, message, 0, unroll=4)
+    pl.semaphore_wait(barrier, peers)
+
     def send_meta(t, _):
         send_group(count - 1 - t, meta_ref, meta_in, meta_s, meta_r)
         return 0
@@ -128,23 +139,43 @@
     lax.fori_loop(0, count, send_meta, 0)
 
     def send_root(t, _):
-        send_group(count - 1 - t, root_ref, root_in, even_s, even_r)
+        far = count - 1 - t
+        g = either(own_group, far, count)
+        alive = jnp.zeros((1, LANES), F32)
+        for j in range(group):
+            there = (spot >= j * cap) & (spot < j * cap + counts_ref[0, g * group + j])
+            alive = jnp.where(there, 1.0, alive)
+        live_ref[pl.ds(g, 1), :] = alive
+        heavy = weight_ref[pl.ds(g, 1), :] * alive
+        wide[g] = column(heavy)
+        at = pl.ds(pl.multiple_of(g * LANES, LANES), LANES)
+        value = jnp.sqrt(heavy) * sketch_ref[:, at].astype(F32)
+        value = jnp.concatenate([value, value], axis=0).T
+        total[g] = value
+        for j in range(group):
+            a = value[j * cap : j * cap + cap // 2]
+            b = value[j * cap + cap // 2 : (j + 1) * cap]
+            root_ref[g * group + j] = jnp.where(mask(a), a, b)
+        send_group(far, root_ref, root_in, even_s, even_r)
         return 0
 
     lax.fori_loop(0, count, send_root, 0)
 
     def first_ends(g, _):
-        row = src_ref[pl.ds(g, 1), :]
+        row = src_ref[pl.ds(g, 1), :].astype(F32)
         rows[g, 0:1] = row
         ids[g] = column(row)
-        wide[g] = column(weight_ref[pl.ds(g, 1), :])
-        return 0
-
-    lax.fori_loop(0, count, first_ends, 0)
-
-    def second_ends(t, _):
-        g, far = near_first(t)
-        wait_group(far, meta_ref, meta_in, meta_s, meta_r)
+        return 0
+
+    lax.fori_loop(0, count, first_ends, 0, unroll=4)
+
+    def take_meta(t, _):
+        wait_group(t, meta_ref, meta_in, meta_s, meta_r)
+        return 0
+
+    lax.fori_loop(0, count, take_meta, 0)
+
+    def second_ends(g, _):
         named = [column(meta_in[g * group + j][0:1])[:cap] for j in range(group)]
         named = jnp.concatenate(named, axis=0)
         heavy = [column(meta_in[g * group + j][1:2])[:cap] for j in range(group)]
@@ -154,7 +185,7 @@
         wide[count + g] = heavy
         return 0
 
-    lax.fori_loop(0, count, second_ends, 0)
+    lax.fori_loop(0, count, second_ends, 0, unroll=4)
 
     tile = 512
     blocks = tile // LANES
@@ -165,22 +196,19 @@
     def first_product(t, _):
         g, far = near_first(t)
         wait_group(far, root_ref, root_in, even_s, even_r)
-        value = jnp.concatenate([split(unfold(root_ref, g)), split(-unfold(root_in, g))], axis=0)
+        value = jnp.concatenate([split(total[g]), split(-unfold(root_in, g))], axis=0)
         load = jnp.concatenate([split(wide[g]), split(wide[count + g])], axis=0)
         x = jnp.concatenate([value, load], axis=1)
         row_u, row_v = rows[g, 0:1], rows[g, 1:2]
 
-        def step(k, _):
-            at = pl.ds(pl.multiple_of(k * tile, tile), tile)
+        for k in range(tiles):
+            at = pl.ds(k * tile, tile)
             name = ids[pl.ds(k * blocks, blocks)].reshape(tile, LANES)
             e = jnp.concatenate(
                 [jnp.where(name == row_u, 1.0, 0.0), jnp.where(name == row_v, 1.0, 0.0)], axis=1
             ).astype(BF16)
             same[g, at, :] = e
             acc[at, :] += jnp.dot(e, x, preferred_element_type=F32)
-            return 0
-
-        lax.fori_loop(0, tiles, step, 0)
         return 0
 
     lax.fori_loop(0, count, first_product, 0)
@@ -222,12 +250,9 @@
             flow_u, flow_v = doubled(flow)
             x = jnp.concatenate([split(flow_u), split(flow_v)], axis=0)
 
-            def step(k, _):
-                at = pl.ds(pl.multiple_of(k * tile, tile), tile)
+            for k in range(tiles):
+                at = pl.ds(k * tile, tile)
                 acc[at, 0:LANES] += jnp.dot(same[g, at, :], x, preferred_element_type=F32)
-                return 0
-
-            lax.fori_loop(0, tiles, step, 0)
             return 0
 
         lax.fori_loop(0, count, product, 0)
@@ -272,9 +297,10 @@
             last_out[g * group + j] = jnp.where(mask(a), turned(a), b)
         send_group(far, last_out, last_in, odd_s, odd_r)
         whole_u, whole_v = doubled(whole)
-        ones = jnp.ones((LANES, LANES), BF16)
-        ends[g, 0:LANES, :] = jnp.concatenate([split(whole_u), ones], axis=1)
-        ends[g, LANES:, :] = jnp.concatenate([split(whole_v), ones], axis=1)
+        ones = jnp.ones((2 * LANES, LANES), BF16)
+        pair = jnp.concatenate([split(whole_u), split(whole_v)], axis=0)
+        at = pl.ds(pl.multiple_of(g * 2 * LANES, 2 * LANES), 2 * LANES)
+        ends[at, :] = jnp.concatenate([pair, ones], axis=1)
         return 0
 
     lax.fori_loop(0, count, third_field, 0)
@@ -284,12 +310,10 @@
     def vertices(k, _):
         first = k * strip
         name = (lax.broadcasted_iota(jnp.int32, (strip, LANES), 0) + first).astype(F32)
-        out = jnp.zeros((strip, 2 * LANES), F32)
-        for g in range(count):
-            e = jnp.concatenate(
-                [jnp.where(name == rows[g, 0:1], 1.0, 0.0), jnp.where(name == rows[g, 1:2], 1.0, 0.0)], axis=1
-            ).astype(BF16)
-            out = out + jnp.dot(e, ends[g], preferred_element_type=F32)
+        e = [
+            jnp.where(name == rows[g, j : j + 1], 1.0, 0.0).astype(BF16) for g in range(count) for j in range(2)
+        ]
+        out = jnp.dot(jnp.concatenate(e, axis=1), ends[...], preferred_element_type=F32)
         value = out[:, 0:LANES]
         value = (value + turned(value)) / jnp.maximum(out[:, LANES:], 1.0)
         sol_ref[:, pl.ds(pl.multiple_of(first, strip), strip)] = value.T[0:HALF]
@@ -322,12 +346,6 @@
     cap = edges // peers
     width = sketch.shape[0]
     count = edges // LANES
-    live = (jnp.arange(cap)[None, :] < send_counts.reshape(peers, 1)).astype(F32)
-    weight = edge_weight.reshape(peers, cap) * live
-    root = (jnp.sqrt(weight).reshape(1, edges) * sketch.astype(F32)).reshape(width, peers, 2, cap // 2)
-    root = root.transpose(1, 3, 2, 0).reshape(peers, cap // 2, LANES)
-    meta = jnp.stack([dst_local.reshape(peers, cap).astype(F32), weight], axis=1)
-    meta = jnp.pad(meta, ((0, 0), (0, 6), (0, LANES - cap)))
     vmem = functools.partial(pl.BlockSpec, memory_space=pltpu.VMEM)
     dma = pltpu.SemaphoreType.DMA
     wide = pltpu.VMEM((count, LANES, LANES), F32)
@@ -336,7 +354,7 @@
     solution, resistance = pl.pallas_call(
         functools.partial(kernel, peers, cap),
         out_shape=(jax.ShapeDtypeStruct((width, VERT_DEV), F32), jax.ShapeDtypeStruct((count, LANES), F32)),
-        in_specs=[vmem()] * 5,
+        in_specs=[pl.BlockSpec(memory_space=pltpu.SMEM)] + [vmem()] * 5,
         out_specs=(vmem(), vmem()),
         scratch_shapes=[
             pltpu.VMEM((count, 2 * edges, 2 * LANES), BF16),
@@ -345,9 +363,12 @@
             pltpu.VMEM((2 * edges, 2 * LANES), F32),
             whole, wide, wide, wide, wide,
             pltpu.VMEM((2 * count, LANES, LANES), F32),
-            pltpu.VMEM((count, 2 * LANES, 2 * LANES), BF16),
+            pltpu.VMEM((2 * edges, 2 * LANES), BF16),
             pltpu.VMEM((count, LANES), F32),
             pltpu.VMEM((count, LANES), F32),
+            pltpu.VMEM((count, LANES), F32),
+            pltpu.VMEM((peers, 8, LANES), F32),
+            half,
             pltpu.VMEM((peers, 8, LANES), F32),
             half, whole, whole, half, half,
             dma((peers,)), dma((peers,)), dma((peers,)), dma((peers,)), dma((peers,)), dma((peers,)),
@@ -356,7 +377,10 @@
         compiler_params=pltpu.CompilerParams(
             collective_id=0, has_side_effects=True, vmem_limit_bytes=60 * 1024 * 1024
         ),
-    )(meta, root, src_local.astype(F32).reshape(count, LANES), weight.reshape(count, LANES), live.reshape(count, LANES))
+    )(
+        send_counts, src_local.reshape(count, LANES), dst_local.reshape(peers, cap),
+        edge_weight.reshape(peers, cap), edge_weight.reshape(count, LANES), sketch,
+    )
     return solution, resistance.reshape(edges)
 
 

time: 173 us -> 123 us (0.71)
  Pallas kernels: 159 us -> 119 us
  local copies, waits for them, and re-layouts: 7.92 us -> 2.88 us
  other arithmetic: 4.42 us -> 0 us
    pallas_call x1, Pallas kernels: 159 us -> 119 us  [local(): pl.pallas_call(functools.partial(kernel, peers, cap), out_shape=(jax.Shap...]
    reshape x3 -> x0, local copies, waits for them, and re-layouts: 3.74 us -> none  [the longest x2 2.35 us: local(): (jnp.sqrt(weight).reshape(1, edges) * sketch.astype(F32)).reshape(width,...]
    mul x3 -> x0, other arithmetic: 1.74 us -> none  [the longest x1 0.99 us: local(): jnp.sqrt(weight).reshape(1, edges) * sketch.astype(F32)]
    unnamed x12 -> x4, local copies, waits for them, and re-layouts: 4.17 us -> 2.88 us
where the time goes in v2:
time: 123 us
  Pallas kernels  119 us (97%)
  local copies, waits for them, and re-layouts  2.88 us (2%)
    pallas_call x1, Pallas kernels, local(): pl.pallas_call(functools.partial(kernel, peers, cap), out_shape=(jax.Shap...  119 us
    unnamed x4, local copies, waits for them, and re-layouts  2.88 us

profile of v2, /device:TPU:0, one launch (start us, length us, event | category | flops | bytes accessed | tf_op | source)
XLA Modules:
  0.0 122.7 jit_solution(15995711493106941509)
XLA Ops:
  0.6 119.2 %shard_map.68 = (f32[64,4096]{1,0:T(8,128)}, f32[16,128]{1,0:T(8,128)}) custom-call(s32[1,16]{1,0:T(1,128)} %counts_ref.1, s32[16,128]{1,0:T(8,128)} %bitcast.6, s32[16,128]{1,0:T(8,128)} %bitcast.7, f32[16,128]{1,0:T(8,128)} %bitcast.4, f32[16,128]{1,0:T(8,128)} %bitcast.5, bf16[64,2048]{1,0:T(8,128)(2,1)} %sketch_ref.1), custom_call_target="tpu_custom_call" | custom-call | tf_op jit(solution)/shard_map/pallas_call | solution.py:354
  119.8 0.0 copy-start
  119.8 2.3 %copy.9 = f32[64,4096]{1,0:T(8,128)} copy(f32[64,4096]{1,0:T(8,128)} %get-tuple-element.8) | data formatting | bytes 2097152
  122.1 0.0 copy-done
  122.1 0.6 copy.10
Async XLA Ops:
  119.8 2.3 %copy-start = (f32[16,128]{1,0:T(8,128)S(1)}, f32[16,128]{1,0:T(8,128)}, u32[]{:S(2)}) copy-start(f32[16,128]{1,0:T(8,128)} %get-tuple-element.5) | copy-start | bytes 24580

commit v3 on v2

--- a/solution.py
+++ b/solution.py
@@ -108,6 +108,13 @@
     def column(row):
         return jnp.broadcast_to(row, (LANES, LANES)).T
 
+    def short(a):
+        return a.astype(jnp.int32).astype(jnp.int16)
+
+    def equal(name, row):
+        row = short(jnp.broadcast_to(row, (LANES, LANES)))
+        return jnp.where(name == row[None], jnp.array(1, BF16), jnp.array(0, BF16)).reshape(-1, LANES)
+
     def unfold(ref, g):
         pieces = []
         for j in range(group):
@@ -164,7 +171,7 @@
     def first_ends(g, _):
         row = src_ref[pl.ds(g, 1), :].astype(F32)
         rows[g, 0:1] = row
-        ids[g] = column(row)
+        ids[g] = short(column(row))
         return 0
 
     lax.fori_loop(0, count, first_ends, 0, unroll=4)
@@ -180,7 +187,7 @@
         named = jnp.concatenate(named, axis=0)
         heavy = [column(meta_in[g * group + j][1:2])[:cap] for j in range(group)]
         heavy = jnp.concatenate(heavy, axis=0)
-        ids[count + g] = named
+        ids[count + g] = short(named)
         rows[g, 1:2] = named.T[0:1]
         wide[count + g] = heavy
         return 0
@@ -203,10 +210,8 @@
 
         for k in range(tiles):
             at = pl.ds(k * tile, tile)
-            name = ids[pl.ds(k * blocks, blocks)].reshape(tile, LANES)
-            e = jnp.concatenate(
-                [jnp.where(name == row_u, 1.0, 0.0), jnp.where(name == row_v, 1.0, 0.0)], axis=1
-            ).astype(BF16)
+            name = ids[pl.ds(k * blocks, blocks)]
+            e = jnp.concatenate([equal(name, row_u), equal(name, row_v)], axis=1)
             same[g, at, :] = e
             acc[at, :] += jnp.dot(e, x, preferred_element_type=F32)
         return 0
@@ -358,7 +363,7 @@
         out_specs=(vmem(), vmem()),
         scratch_shapes=[
             pltpu.VMEM((count, 2 * edges, 2 * LANES), BF16),
-            pltpu.VMEM((2 * count, LANES, LANES), F32),
+            pltpu.VMEM((2 * count, LANES, LANES), jnp.int16),
             pltpu.VMEM((count, 8, LANES), F32),
             pltpu.VMEM((2 * edges, 2 * LANES), F32),
             whole, wide, wide, wide, wide,

time: 123 us -> 121 us (0.984)
  Pallas kernels: 119 us -> 117 us
    pallas_call x1, Pallas kernels: 119 us -> 117 us  [local(): pl.pallas_call(functools.partial(kernel, peers, cap), out_shape=(jax.Shap...]
where the time goes in v3:
time: 121 us
  Pallas kernels  117 us (97%)
  local copies, waits for them, and re-layouts  2.88 us (2%)
    pallas_call x1, Pallas kernels, local(): pl.pallas_call(functools.partial(kernel, peers, cap), out_shape=(jax.Shap...  117 us
    unnamed x4, local copies, waits for them, and re-layouts  2.88 us

profile of v3, /device:TPU:0, one launch (start us, length us, event | category | flops | bytes accessed | tf_op | source)
XLA Modules:
  0.0 120.9 jit_solution(9385644937100792510)
XLA Ops:
  0.6 117.4 %shard_map.68 = (f32[64,4096]{1,0:T(8,128)}, f32[16,128]{1,0:T(8,128)}) custom-call(s32[1,16]{1,0:T(1,128)} %counts_ref.1, s32[16,128]{1,0:T(8,128)} %bitcast.6, s32[16,128]{1,0:T(8,128)} %bitcast.7, f32[16,128]{1,0:T(8,128)} %bitcast.4, f32[16,128]{1,0:T(8,128)} %bitcast.5, bf16[64,2048]{1,0:T(8,128)(2,1)} %sketch_ref.1), custom_call_target="tpu_custom_call" | custom-call | tf_op jit(solution)/shard_map/pallas_call | solution.py:359
  118.0 0.0 copy-start
  118.0 2.3 %copy.9 = f32[64,4096]{1,0:T(8,128)} copy(f32[64,4096]{1,0:T(8,128)} %get-tuple-element.8) | data formatting | bytes 2097152
  120.3 0.0 copy-done
  120.3 0.6 copy.10
Async XLA Ops:
  118.0 2.3 %copy-start = (f32[16,128]{1,0:T(8,128)S(1)}, f32[16,128]{1,0:T(8,128)}, u32[]{:S(2)}) copy-start(f32[16,128]{1,0:T(8,128)} %get-tuple-element.5) | copy-start | bytes 24580
